TPU v7x, 32 devices: a whole 2x2x4 slice. The times are simulated.
32 devices in a mesh: row: 4 (over y, core), col: 8 (over z, x).
Axes of the slice: x: 2, y: 2, z: 4, core: 2. Of those that a mesh axis runs over, the one named last changes fastest.
Arguments:
- row_coords: bfloat16 [3, 4096, 512], P(None, ('row', 'col')), may hold values from -10 to 10, as said below
- col_coords: bfloat16 [3, 8192, 512], P(None, 'col'), may hold values from -10 to 10, as said below
- start_block: float32 [8192, 64], P('col'), may hold values from -0.0625 to 0.0625
Outputs:
- basis: float32 [4096, 64], P('row')
- image: float32 [8192, 64], P('col')
Inputs may be any that keep to these rules, and one draw needn't show every extreme that they name: `row_coords`: coordinates of frames of one molecule in varying conformations. `col_coords`: coordinates of frames of the same molecule in varying conformations.
All inputs are finite; a program needn't handle non-finite values.
Results may differ from a plain program's by a relative error of at most 0.0073.
Values may be sent and summed in bfloat16 or wider, within the bound.
A program may use at most 128 MiB of HBM per device.

v0:
```python
import math

import jax
import jax.numpy as jnp
from jax import lax
from jax.sharding import PartitionSpec as P

ATOMS = 512
NEWTON = 8


def centre_frames(coords):
    shifted = coords.astype(jnp.float32)
    shifted = shifted - jnp.mean(shifted, axis=2, keepdims=True)
    rounded = shifted.astype(jnp.bfloat16)
    widened = lax.optimization_barrier(rounded).astype(jnp.float32)
    return (rounded, jnp.sum(widened * widened, axis=(0, 2)) / ATOMS)


def two_minor(matrix, upper, lower, left, right):
    return matrix[upper][left] * matrix[lower][right] - matrix[lower][left] * matrix[upper][right]


def squared_rmsd(cross, row_norm, col_norm):
    part = [[cross[first, second] for second in range(3)] for first in range(3)]
    trace = part[0][0] + part[1][1] + part[2][2]
    matrix = [[None] * 4 for index in range(4)]
    matrix[0][0] = trace
    matrix[1][1] = 2.0 * part[0][0] - trace
    matrix[2][2] = 2.0 * part[1][1] - trace
    matrix[3][3] = 2.0 * part[2][2] - trace
    matrix[0][1] = part[1][2] - part[2][1]
    matrix[0][2] = part[2][0] - part[0][2]
    matrix[0][3] = part[0][1] - part[1][0]
    matrix[1][2] = part[0][1] + part[1][0]
    matrix[1][3] = part[2][0] + part[0][2]
    matrix[2][3] = part[1][2] + part[2][1]
    for first in range(4):
        for second in range(first):
            matrix[first][second] = matrix[second][first]
    key_determinant = (
        two_minor(matrix, 0, 1, 0, 1) * two_minor(matrix, 2, 3, 2, 3)
        - two_minor(matrix, 0, 1, 0, 2) * two_minor(matrix, 2, 3, 1, 3)
        + two_minor(matrix, 0, 1, 0, 3) * two_minor(matrix, 2, 3, 1, 2)
        + two_minor(matrix, 0, 1, 1, 2) * two_minor(matrix, 2, 3, 0, 3)
        - two_minor(matrix, 0, 1, 1, 3) * two_minor(matrix, 2, 3, 0, 2)
        + two_minor(matrix, 0, 1, 2, 3) * two_minor(matrix, 2, 3, 0, 1)
    )
    cross_determinant = (
        part[0][0] * (part[1][1] * part[2][2] - part[1][2] * part[2][1])
        - part[0][1] * (part[1][0] * part[2][2] - part[1][2] * part[2][0])
        + part[0][2] * (part[1][0] * part[2][1] - part[1][1] * part[2][0])
    )
    squares = sum(
        (part[first][second] * part[first][second] for first in range(3) for second in range(3))
    )
    coeff_two = -2.0 * squares
    coeff_one = -8.0 * cross_determinant
    root_guess = 0.5 * (row_norm + col_norm)
    for sweep in range(NEWTON):
        poly_value = (
            (root_guess * root_guess + coeff_two) * root_guess + coeff_one
        ) * root_guess + key_determinant
        poly_slope = (4.0 * root_guess * root_guess + 2.0 * coeff_two) * root_guess + coeff_one
        root_guess = root_guess - poly_value / poly_slope
    return row_norm + col_norm - 2.0 * root_guess


def body(row_coords, col_coords, start_block):
    highest = lax.Precision.HIGHEST
    cols, col_norm = centre_frames(col_coords)
    rows, row_norm = centre_frames(lax.all_gather(row_coords, "col", axis=1, tiled=True))
    cross = jnp.einsum("ark,bck->abrc", rows, cols, preferred_element_type=jnp.float32) / ATOMS
    dist = squared_rmsd(cross, row_norm[:, None], col_norm[None, :])
    row_count, col_count = dist.shape
    total_rows = row_count * lax.axis_size("row")
    total_cols = col_count * lax.axis_size("col")
    block_mean = lax.psum(jnp.sum(start_block, axis=0), "col") / total_cols
    panel_terms = (
        jnp.dot(dist, start_block - block_mean[None, :], precision=highest),
        jnp.sum(dist, axis=1),
    )
    summed = lax.psum((panel_terms[0], panel_terms[1]), "col")
    product = summed[0]
    stats = lax.psum(
        (jnp.dot(product.T, product, precision=highest), jnp.sum(product, axis=0)), "row"
    )
    mean_row = stats[1] / total_rows
    panel = -0.5 * (summed[0] - mean_row[None, :])
    gram = 0.25 * (stats[0] / total_rows - jnp.outer(mean_row, mean_row))
    lower = jnp.linalg.cholesky(gram)
    basis = lax.linalg.triangular_solve(lower, panel, left_side=False, lower=True, transpose_a=True)
    row_totals = summed[1]
    column_terms = (
        jnp.dot(dist.T, basis, precision=highest),
        jnp.dot(row_totals, basis, precision=highest),
    )
    reduced = lax.psum((column_terms[0], column_terms[1]), "row")
    image = -0.5 * (reduced[0] - reduced[1][None, :] / total_cols) / math.sqrt(total_rows)
    return (basis, image)


def solution(mesh):
    in_specs = (P(None, ("row", "col"), None), P(None, "col", None), P("col", None))
    out_specs = (P("row", None), P("col", None))
    return jax.shard_map(body, mesh=mesh, in_specs=in_specs, out_specs=out_specs, check_vma=False)
```

profile of v0, /device:TPU:25, one launch (start us, length us, event | category | flops | bytes accessed | tf_op | source)
XLA Modules:
  0.0 300.2 jit_solution(3757768038669718593)
XLA Ops:
  7.2 0.0 copy-start
  7.2 0.0 all-gather.2.cloned.1.call-start
  7.2 0.7 all-gather.2.cloned.1.call-update
  7.9 0.0 copy-start.4
  7.9 0.0 all-reduce.5.cloned.1.call-start
  8.0 2.6 convert_reduce_fusion
  10.6 0.0 copy-done
  10.6 2.1 fusion.7
  12.7 0.0 copy-done.4
  12.7 0.1 reduce_sum.67
  12.8 2.6 multiply_reduce_fusion
  15.4 55.0 %all-gather.2.cloned.1.call-done = bf16[3,1024,512]{2,1,0:T(8,128)(2,1)} async-done(((bf16[3,128,512]{2,1,0:T(8,128)(2,1)}), bf16[3,1024,512]{2,1,0:T(8,128)(2,1)}) %all-gather.2.cloned.1.call-update) | async-done | bytes 3145744 | tf_op jit(solution)/shard_map/all_gather | solution.py:72
  70.4 0.0 copy-start.1
  70.4 0.0 copy-start.2
  70.4 2.5 convert_reduce_fusion.1
  72.9 0.3 copy-done.1
  73.2 0.8 fusion.6
  74.0 0.2 copy-done.2
  74.2 16.0 %multiply_bitcast_fusion = f32[3,3,1024,1024]{2,3,0,1:T(8,128)} fusion(bf16[3,1024,512]{2,1,0:T(8,128)(2,1)S(1)} %copy-done.2, bf16[3,1024,512]{2,1,0:T(8,128)(2,1)S(1)} %fusion.6), kind=kOutput, calls=%fused_computation | convolution fusion | flops 9673113600 | bytes 44040192 | tf_op jit(solution)/shard_map/ark,bck->abrc/dot_general | solution.py:73
  90.2 0.7 multiply_reduce_fusion.1
  90.9 36.2 %fusion.65 = (f32[1024]{0:T(1024)S(1)}, f32[1024,1024]{0,1:T(8,128)}) fusion(f32[3,3,1024,1024]{2,3,0,1:T(8,128)} %multiply_bitcast_fusion, f32[1024]{0:T(1024)S(1)} %broadcast_multiply_fusion.2, f32[1024]{0:T(1024)S(1)} %broadcast_multiply_fusion.3), kind=kLoop, calls=%fused_computation.111 | loop fusion | flops 210762752 | bytes 41955328 | tf_op jit(solution)/shard_map/reduce_sum | solution.py:81
  127.1 12.4 %all-reduce = (f32[64]{0:T(128)S(1)}, f32[1024]{0:T(1024)S(1)}) all-reduce(f32[64]{0:T(128)S(1)} %reduce_sum.67, f32[1024]{0:T(1024)S(1)} %get-tuple-element.6), channel_id=1, replica_groups=mesh['row'=4,'col'=8] {'col'}, use_global_device_ids=true, to_apply=%region_5.0 | all-reduce | flops 1088 | bytes 8704 | tf_op jit(solution)/shard_map/psum | solution.py:78
  139.5 5.7 %fusion.56 = f32[1024,64]{0,1:T(8,128)} fusion(f32[1024,1024]{0,1:T(8,128)} %get-tuple-element.7, f32[1024,64]{0,1:T(8,128)S(1)} %copy-done.4, f32[64]{0:T(128)S(1)} %broadcast_multiply_fusion.6), kind=kOutput, calls=%fused_computation.88 | convolution fusion | flops 805371904 | bytes 4718848 | tf_op jit(solution)/shard_map/dot_general | solution.py:80
  145.3 0.0 all-reduce.5.cloned.1.call-update
  145.3 0.2 all-reduce.7.cloned.1.call-start
  145.5 73.1 %all-reduce.5.cloned.1.call-done = f32[1024,64]{0,1:T(8,128)} async-done(((f32[1024,64]{0,1:T(8,128)}), f32[1024,64]{0,1:T(8,128)}) %all-reduce.5.cloned.1.call-update) | async-done | bytes 262160 | tf_op jit(solution)/shard_map/psum | solution.py:83
  218.6 1.4 fusion.66
  220.0 1.1 reduce_sum.68
  221.1 12.6 %all-reduce.1 = (f32[64]{0:T(128)S(1)}, f32[64,64]{0,1:T(8,128)S(1)}) all-reduce(f32[64]{0:T(128)S(1)} %reduce_sum.68, f32[64,64]{0,1:T(8,128)S(1)} %fusion.66), channel_id=1, replica_groups=mesh['row'=4,'col'=8] {'row'}, use_global_device_ids=true, to_apply=%region_8.0 | all-reduce | flops 4160 | bytes 33280 | tf_op jit(solution)/shard_map/psum | solution.py:85
  233.7 0.1 subtract_multiply_fusion.1
  233.8 0.1 copy.14
  233.9 0.1 fusion.63
  234.0 5.8 %cholesky.16 = f32[64,64]{1,0:T(8,128)S(1)} custom-call(f32[64,64]{1,0:T(8,128)S(1)} %fusion.63), custom_call_target="Cholesky" | custom-call | tf_op jit(solution)/shard_map/jit(cholesky)/cholesky | solution.py:91
  239.8 0.6 compare_reduce_fusion
  240.5 0.7 fusion.61
  241.1 4.9 %custom-call.6 = f32[1,64,64]{1,2,0:T(8,128)S(1)} custom-call(f32[1,64,64]{2,1,0:T(8,128)S(1)} %fusion.61), custom_call_target="InvertDiagBlocksLowerTriangular" | custom-call | tf_op jit(solution)/shard_map/triangular_solve | solution.py:92
  246.0 1.4 fusion.53
  247.5 0.0 copy-start.3
  247.5 7.1 %fusion.67 = f32[1024,64]{0,1:T(8,128)} fusion(f32[1024,1024]{0,1:T(8,128)} %get-tuple-element.7, f32[1024,64]{0,1:T(8,128)S(1)} %fusion.53), kind=kOutput, calls=%fused_computation.113 | convolution fusion | flops 805306368 | bytes 4718592 | tf_op jit(solution)/shard_map/dot_general | solution.py:95
  254.6 0.3 convolution_bitcast_fusion
  254.9 5.5 %psum.55 = f32[64]{0:T(128)S(1)} all-reduce(f32[64]{0:T(128)S(1)} %convolution_bitcast_fusion), channel_id=1, replica_groups=mesh['row'=4,'col'=8] {'row'}, use_global_device_ids=true, to_apply=%region_15.16 | all-reduce | flops 64 | bytes 512 | tf_op jit(solution)/shard_map/psum | solution.py:98
  260.4 0.0 all-reduce.7.cloned.1.call-update
  260.4 31.5 %all-reduce.7.cloned.1.call-done = f32[1024,64]{0,1:T(8,128)} async-done(((f32[1024,64]{0,1:T(8,128)}), f32[1024,64]{0,1:T(8,128)}) %all-reduce.7.cloned.1.call-update) | async-done | bytes 262160 | tf_op jit(solution)/shard_map/psum | solution.py:98
  291.9 1.7 subtract_multiply_fusion
  293.7 0.0 copy-done.3
  (8 shorter events, 0.1 us)
Async XLA Ops:
  7.2 3.4 %copy-start = (bf16[3,1024,512]{2,1,0:T(8,128)(2,1)S(1)}, bf16[3,1024,512]{2,1,0:T(8,128)(2,1)}, u32[]{:S(2)}) copy-start(bf16[3,1024,512]{2,1,0:T(8,128)(2,1)} %param.4) | copy-start | bytes 9437188
  7.2 63.2 %all-gather.2.cloned.1.call-start = ((), (), s32[]{:S(2)}) async-start(), calls=%async_computation | async-start | bytes 3538944 | tf_op jit(solution)/shard_map/all_gather | solution.py:72
  7.9 4.8 %copy-start.4 = (f32[1024,64]{0,1:T(8,128)S(1)}, f32[1024,64]{0,1:T(8,128)}, u32[]{:S(2)}) copy-start(f32[1024,64]{0,1:T(8,128)} %param.5) | copy-start | bytes 786436
  7.9 210.7 %all-reduce.5.cloned.1.call-start = ((), (), s32[]{:S(2)}) async-start(), calls=%async_computation.1 | async-start | bytes 524288 | tf_op jit(solution)/shard_map/psum | solution.py:83
  70.4 2.8 copy-start.1
  70.4 3.8 %copy-start.2 = (bf16[3,1024,512]{2,1,0:T(8,128)(2,1)S(1)}, bf16[3,1024,512]{2,1,0:T(8,128)(2,1)}, u32[]{:S(2)}) copy-start(bf16[3,1024,512]{2,1,0:T(8,128)(2,1)} %fusion.7) | copy-start | bytes 9437188
  145.3 146.6 %all-reduce.7.cloned.1.call-start = ((), (), s32[]{:S(2)}) async-start(), calls=%async_computation.2 | async-start | bytes 524288 | tf_op jit(solution)/shard_map/psum | solution.py:98
  247.5 46.2 %copy-start.3 = (f32[1024,64]{0,1:T(8,128)}, f32[1024,64]{0,1:T(8,128)S(1)}, u32[]{:S(2)}) copy-start(f32[1024,64]{0,1:T(8,128)S(1)} %fusion.53) | copy-start | bytes 786436
Sparse Core Ops, SparseCore 0:
  10.2 60.1 all-gather.1
  145.4 73.1 all-reduce.4
  260.6 31.3 all-reduce.6
where the time goes:
time: 303 us; the launch traced here: 300 us
  waiting for transfers between devices  160 us (53%)
  other arithmetic  62.7 us (21%)
  matrix products  31.9 us (11%)
  blocking collectives  30.5 us (10%)
  between operations  13.9 us (5%)
    psum x1, waiting for transfers between devices, body(): summed = lax.psum((panel_terms[0], panel_terms[1]), 'col')  73.1 us
    all_gather x1, waiting for transfers between devices, body(): lax.all_gather(row_coords, 'col', axis=1, tiled=True)  55 us
    reduce_sum x1, other arithmetic, body(): jnp.sum(dist, axis=1)  36.2 us
    psum x1, waiting for transfers between devices, body(): reduced = lax.psum((column_terms[0], column_terms[1]), 'row')  31.5 us
    dot_general x1, matrix products, body(): jnp.einsum('ark,bck->abrc', rows, cols, preferred_element_type=jnp.float32)  16 us
    psum x1, blocking collectives, body(): lax.psum((jnp.dot(product.T, product, precision=highest), jnp.sum(product...  12.6 us
    psum x1, blocking collectives, body(): block_mean = lax.psum(jnp.sum(start_block, axis=0), 'col') / total_cols  12.4 us
    dot_general x1, matrix products, body(): jnp.dot(dist.T, basis, precision=highest)  7.14 us
  transfers between devices with their start and end apart: 3, of which 3 were waited for; matrix products, arithmetic and copies ran while one was open for 2% of the time, Pallas kernels for 0%

commit v1 on v0

v1 whole, which is shorter than its diff:
```python
import functools
import math

import jax
import jax.numpy as jnp
from jax import lax
from jax.experimental import pallas as pl
from jax.experimental.pallas import tpu as pltpu
from jax.sharding import PartitionSpec as P

NEWTON = 8
TILE = 256
MESH = pl.DeviceIdType.MESH
HIGHEST = lax.Precision.HIGHEST
F32, BF16 = jnp.float32, jnp.bfloat16


def dot_nt(left, right, precision=None):
    return lax.dot_general(
        left, right, (((1,), (1,)), ((), ())), precision=precision, preferred_element_type=F32
    )


def dot_nn(left, right, precision=None):
    return lax.dot_general(
        left, right, (((1,), (0,)), ((), ())), precision=precision, preferred_element_type=F32
    )


def split(value):
    high = value.astype(BF16)
    return high, (value - high.astype(F32)).astype(BF16)


def setup_terms(s):
    c00 = s[1][1] * s[2][2] - s[1][2] * s[2][1]
    c01 = s[1][2] * s[2][0] - s[1][0] * s[2][2]
    c02 = s[1][0] * s[2][1] - s[1][1] * s[2][0]
    c10 = s[2][1] * s[0][2] - s[2][2] * s[0][1]
    c11 = s[2][2] * s[0][0] - s[2][0] * s[0][2]
    c12 = s[2][0] * s[0][1] - s[2][1] * s[0][0]
    c20 = s[0][1] * s[1][2] - s[0][2] * s[1][1]
    c21 = s[0][2] * s[1][0] - s[0][0] * s[1][2]
    c22 = s[0][0] * s[1][1] - s[0][1] * s[1][0]
    det = s[0][0] * c00 + s[0][1] * c01 + s[0][2] * c02
    square = lambda items: functools.reduce(lambda a, b: a + b, [v * v for v in items])
    total = square([s[a][b] for a in range(3) for b in range(3)])
    cof = square([c00, c01, c02, c10, c11, c12, c20, c21, c22])
    return total, cof, -2.0 * det


def distances(items):
    coeffs = [setup_terms(s) for s, _, _ in items]
    sums = [rn + cn for _, rn, cn in items]
    lam = [0.5 * v for v in sums]
    for _ in range(NEWTON):
        for k, (total, cof, g) in enumerate(coeffs):
            x = lam[k]
            m = x * x - total
            value = 0.25 * (m * m) + (g * x - cof)
            lam[k] = x - value * pl.reciprocal(m * x + g, approx=True)
    return [v - 2.0 * x for v, x in zip(sums, lam)]


def kernel(n, nr, total_rows, total_cols, row_ref, col_ref, st_ref, basis_ref, image_ref,
           rbuf, cc, cn_ref, rn_ref, rc, s_a, s_b, d_hi, d_lo, lhs, ssb, pout, part, agb, q_ref, lhs2,
           gx, uout, ub, ib,
           ag_send, ag_recv, ss_send, ss_recv, pa_send, pa_recv, pg_send, pg_recv,
           gx_send, gx_recv, u_send, u_recv, i_send, i_recv):
    c, r = lax.axis_index("col"), lax.axis_index("row")
    line = n // 2
    z, x = c // 2, c % 2
    _, block_rows, atoms = row_ref.shape
    cols = col_ref.shape[1]
    vecs = st_ref.shape[0]
    chunk = cols // nr
    tiles = cols // TILE

    def col_dev(k):
        return (r, k)

    def row_dev(k):
        return (k, c)

    def remote(src, dst, send, recv, dev):
        return pltpu.make_async_remote_copy(
            src_ref=src, dst_ref=dst, send_sem=send, recv_sem=recv, device_id=dev, device_id_type=MESH
        )

    barrier = pltpu.get_barrier_semaphore()
    for d in range(1, n):
        pl.semaphore_signal(barrier, inc=1, device_id=col_dev((c + d) % n), device_id_type=MESH)
    for d in range(1, nr):
        pl.semaphore_signal(barrier, inc=1, device_id=row_dev((r + d) % nr), device_id_type=MESH)
    rbuf[c] = row_ref[...]
    pl.semaphore_wait(barrier, n - 1 + nr - 1)

    def hop(block, way):
        dev = col_dev((c + 1 - 2 * x, c + 2, c - 2)[way])
        return remote(rbuf.at[block], rbuf.at[block], ag_send.at[way, block], ag_recv.at[block], dev)

    def hops(block_z, act):
        block = block_z * 2 + x
        act(hop(block, 0))

        @pl.when((block_z <= z) & (z < line - 1))
        def _():
            act(hop(block, 1))

        @pl.when((block_z >= z) & (z > 0))
        def _():
            act(hop(block, 2))

    hops(z, lambda copy: copy.start())

    st = st_ref[...]
    st_hi, st_lo = split(st)
    lhs[0:vecs, :] = st_hi
    lhs[vecs:2 * vecs, :] = st_lo
    lhs[2 * vecs:2 * vecs + 16, :] = jnp.ones((16, cols), BF16)
    ssb[c] = dot_nt(jnp.ones((8, cols), F32), st, HIGHEST)

    def ss_copy(d):
        k = (c + d) % n
        return remote(ssb.at[c], ssb.at[c], ss_send.at[d], ss_recv.at[c], col_dev(k))

    for d in range(1, n):
        ss_copy(d).start()

    step_rows = 128

    def centre_cols(k, carry):
        at = pl.ds(pl.multiple_of(k * step_rows, step_rows), step_rows)
        squares = jnp.zeros((step_rows, atoms), F32)
        for b in range(3):
            v = col_ref[b, at, :].astype(F32)
            v = (v - jnp.sum(v, axis=1, keepdims=True) * (1.0 / atoms)).astype(BF16)
            cc[b, at, :] = v
            v = v.astype(F32)
            squares = squares + v * v
        cn_ref[:, at] = dot_nt(jnp.ones((8, atoms), F32), squares, HIGHEST) * (1.0 / atoms)
        return carry

    lax.fori_loop(0, cols // step_rows, centre_cols, 0)

    near = jnp.minimum(z, line - 1 - z)
    sign = jnp.where(z < line - 1 - z, 1, -1)

    def line_place(q):
        both = jnp.where(q % 2 == 1, (q + 1) // 2, -(q // 2))
        return z + jnp.where(q <= 2 * near, both, sign * (q - near))

    def part_copy(block):
        return remote(pout.at[block], part.at[c], pa_send.at[block], pa_recv.at[c], col_dev(block))

    def run_block(p, carry):
        block_z = line_place(p // 2)
        other = p % 2
        block = block_z * 2 + jnp.where(other == 1, 1 - x, x)

        @pl.when(p > 0)
        def _():
            hop(block, 0).wait_recv()

        @pl.when((p > 0) & (other == 0))
        def _():
            hops(block_z, lambda copy: copy.start())

        norm = jnp.zeros((block_rows, 1), F32)
        for a in range(3):
            v = rbuf[block, a].astype(F32)
            v = (v - jnp.sum(v, axis=1, keepdims=True) * (1.0 / atoms)).astype(BF16).astype(F32)
            norm = norm + jnp.sum(v * v, axis=1, keepdims=True)
            rc[a * block_rows:(a + 1) * block_rows, :] = (v * (1.0 / atoms)).astype(BF16)
        rn_ref[...] = jnp.broadcast_to(norm * (1.0 / atoms), (block_rows, 128))

        def cross(t, out):
            at = pl.ds(pl.multiple_of(t * TILE, TILE), TILE)
            for b in range(3):
                out[b] = dot_nt(rc[...], cc[b, at, :])

        def solve(t, src):
            for i0 in range(0, block_rows, 32):
                items, places = [], []
                for i in range(i0, i0 + 32, 8):
                    rn = rn_ref[i:i + 8, :]
                    for l in range(0, TILE, 128):
                        s = [[src[b, a * block_rows + i:a * block_rows + i + 8, l:l + 128] for b in range(3)]
                             for a in range(3)]
                        cn = cn_ref[:, pl.ds(pl.multiple_of(t * TILE + l, 128), 128)]
                        items.append((s, rn, cn))
                        places.append((i, l))
                dist = dict(zip(places, distances(items)))
                for i in range(i0, i0 + 32, 16):
                    at_rows = pl.ds(pl.multiple_of(block * block_rows + i, 16), 16)
                    for l in range(0, TILE, 128):
                        value = jnp.concatenate([dist[(i, l)], dist[(i + 8, l)]], axis=0)
                        high, low = split(value)
                        at_cols = pl.ds(pl.multiple_of(t * TILE + l, 128), 128)
                        d_hi[at_rows, at_cols] = high
                        d_lo[at_rows, at_cols] = low

        cross(0, s_a)

        def pair(k, inner):
            t = 2 * k
            cross(t + 1, s_b)
            solve(t, s_a)
            cross((t + 2) % tiles, s_a)
            solve(t + 1, s_b)
            return inner

        lax.fori_loop(0, tiles // 2, pair, 0)

        at = pl.ds(pl.multiple_of(block * block_rows, block_rows), block_rows)
        high = dot_nt(lhs[...], d_hi[at, :])
        low = dot_nt(lhs[0:vecs, :], d_lo[at, :])
        low_sum = dot_nt(lhs[2 * vecs:2 * vecs + 16, :], d_lo[at, :])
        pout[block, 0:vecs] = high[0:vecs] + high[vecs:2 * vecs] + low
        pout[block, vecs:vecs + 8] = high[2 * vecs:2 * vecs + 8] + low_sum[0:8]

        @pl.when(block == c)
        def _():
            part[c] = pout[block]

        @pl.when(block != c)
        def _():
            part_copy(block).start()

        return carry

    lax.fori_loop(0, n, run_block, 0)

    for d in range(1, n):
        k = (c + d) % n
        remote(ssb.at[k], ssb.at[k], ss_send.at[d], ss_recv.at[k], col_dev(k)).wait_recv()
        remote(pout.at[k], part.at[k], pa_send.at[k], pa_recv.at[k], col_dev(k)).wait_recv()
    summed, starts = part[0], ssb[0]
    for k in range(1, n):
        summed, starts = summed + part[k], starts + ssb[k]
    eye = lax.broadcasted_iota(jnp.int32, (vecs, vecs), 0) == lax.broadcasted_iota(jnp.int32, (vecs, vecs), 1)
    mean = jnp.sum(jnp.where(eye, jnp.broadcast_to(starts[0:1, :], (vecs, vecs)), 0.0), axis=1, keepdims=True)
    mean = mean * (1.0 / total_cols)
    agb[c, 0:vecs] = summed[0:vecs] - mean * summed[vecs:vecs + 1]
    agb[c, vecs:vecs + 8] = summed[vecs:vecs + 8]

    def pg_copy(d):
        return remote(agb.at[c], agb.at[c], pg_send.at[d], pg_recv.at[c], col_dev((c + d) % n))

    for d in range(1, n):
        pg_copy(d).start()
    for d in range(1, n):
        k = (c + d) % n
        remote(agb.at[k], agb.at[k], pg_send.at[d], pg_recv.at[k], col_dev(k)).wait_recv()

    local = n * block_rows
    for k in range(n):
        q_ref[:, k * block_rows:(k + 1) * block_rows] = agb[k]
    prod = q_ref[0:vecs, :]
    row_total = q_ref[vecs:vecs + 1, :]
    local_mean = jnp.sum(prod, axis=1, keepdims=True) * (1.0 / local)
    q = prod - local_mean
    q_ref[0:vecs, :] = q
    q_hi, q_lo = split(q)
    lhs2[0:vecs, :] = q_hi
    lhs2[vecs:2 * vecs, :] = q_lo
    lhs2[2 * vecs:2 * vecs + 16, :] = jnp.ones((16, local), BF16)
    gx[r, :, 0:vecs] = dot_nt(q, q, HIGHEST)
    lane = lax.broadcasted_iota(jnp.int32, (vecs, 128), 1)
    extra = jnp.where(lane == 0, local_mean, 0.0)
    extra = extra + jnp.where(lane == 1, jnp.sum(q * row_total, axis=1, keepdims=True), 0.0)
    extra = extra + jnp.where(lane == 2, jnp.sum(row_total, axis=1, keepdims=True), 0.0)
    gx[r, :, 128:256] = extra

    def gx_copy(d):
        return remote(gx.at[r], gx.at[r], gx_send.at[d], gx_recv.at[r], row_dev((r + d) % nr))

    for d in range(1, nr):
        gx_copy(d).start()

    def u_copy(d):
        o = (r + d) % nr
        return remote(uout.at[d], ub.at[r], u_send.at[d], u_recv.at[r], row_dev(o))

    for d in list(range(1, nr)) + [0]:
        o = (r + d) % nr
        at = pl.ds(pl.multiple_of(o * chunk, chunk), chunk)
        high = dot_nn(lhs2[...], d_hi[:, at])
        low = dot_nn(lhs2[0:vecs, :], d_lo[:, at])
        low_sum = dot_nn(lhs2[2 * vecs:2 * vecs + 16, :], d_lo[:, at])
        product = high[0:vecs] + high[vecs:2 * vecs] + low
        sums = high[2 * vecs:2 * vecs + 8] + low_sum[0:8]
        if d:
            uout[d, 0:vecs] = product
            uout[d, vecs:vecs + 8] = sums
            u_copy(d).start()
        else:
            ub[r, 0:vecs] = product
            ub[r, vecs:vecs + 8] = sums

    for d in range(1, nr):
        k = (r + d) % nr
        remote(gx.at[k], gx.at[k], gx_send.at[d], gx_recv.at[k], row_dev(k)).wait_recv()
    means = [gx[k, :, 128:129] for k in range(nr)]
    mean = sum(means) * (1.0 / nr)
    shift = jnp.zeros((vecs, 128), F32)
    gram = jnp.zeros((vecs, vecs), F32)
    weighted = jnp.zeros((vecs, 1), F32)
    for k in range(nr):
        gram = gram + gx[k, :, 0:vecs]
        shift = shift + jnp.where(lane == k, means[k] - mean, 0.0)
        weighted = weighted + gx[k, :, 129:130] + (means[k] - mean) * gx[k, :, 130:131]
    gram = (gram + float(local) * dot_nt(shift, shift, HIGHEST)) * (1.0 / total_rows)

    work = jnp.concatenate([gram, jnp.where(eye, 1.0, 0.0)], axis=1)
    below = lax.broadcasted_iota(jnp.int32, (vecs, 1), 0)
    pivots = jnp.zeros((vecs, 1), F32)
    for k in range(vecs):
        top = work[k:k + 1, :]
        pivot = top[:, k:k + 1]
        pivots = jnp.where(below == k, pivot, pivots)
        factor = jnp.where(below > k, work[:, k:k + 1], 0.0)
        work = work - factor * (top * (1.0 / pivot))
    inverse = work[:, vecs:2 * vecs] * lax.rsqrt(pivots)

    own_mean = jnp.sum(jnp.where(lane == r, shift, 0.0), axis=1, keepdims=True)
    basis_ref[...] = -dot_nn(inverse, q_ref[0:vecs, :] + own_mean, HIGHEST)

    for d in range(1, nr):
        k = (r + d) % nr
        remote(uout.at[d], ub.at[k], u_send.at[d], u_recv.at[k], row_dev(k)).wait_recv()
    gathered = jnp.broadcast_to(weighted * (-1.0 / total_cols), (vecs, chunk))
    for k in range(nr):
        gathered = gathered + (ub[k, 0:vecs] + (means[k] - mean) * ub[k, vecs:vecs + 1])
    ib[r] = dot_nn(inverse, gathered, HIGHEST) * (0.5 / math.sqrt(total_rows))

    def i_copy(d):
        return remote(ib.at[r], ib.at[r], i_send.at[d], i_recv.at[r], row_dev((r + d) % nr))

    for d in range(1, nr):
        i_copy(d).start()
    for d in range(1, nr):
        k = (r + d) % nr
        remote(ib.at[k], ib.at[k], i_send.at[d], i_recv.at[k], row_dev(k)).wait_recv()
    for k in range(nr):
        image_ref[:, k * chunk:(k + 1) * chunk] = ib[k]

    for place in range(line):
        hops(place, lambda copy: copy.wait_send())
    for d in range(1, n):
        ss_copy(d).wait_send()
        pg_copy(d).wait_send()
        part_copy((c + d) % n).wait_send()
    for d in range(1, nr):
        gx_copy(d).wait_send()
        u_copy(d).wait_send()
        i_copy(d).wait_send()


def solution(mesh):
    n, nr = mesh.shape["col"], mesh.shape["row"]

    def body(row_coords, col_coords, start_block):
        _, block_rows, atoms = row_coords.shape
        cols, vecs = start_block.shape
        local = n * block_rows
        chunk = cols // nr
        dma = pltpu.SemaphoreType.DMA
        basis, image = pl.pallas_call(
            functools.partial(kernel, n, nr, local * nr, cols * n),
            out_shape=(
                jax.ShapeDtypeStruct((vecs, local), F32),
                jax.ShapeDtypeStruct((vecs, cols), F32),
            ),
            in_specs=[pl.BlockSpec(memory_space=pltpu.VMEM)] * 3,
            out_specs=[pl.BlockSpec(memory_space=pltpu.VMEM)] * 2,
            scratch_shapes=[
                pltpu.VMEM((n, 3, block_rows, atoms), BF16),
                pltpu.VMEM((3, cols, atoms), BF16),
                pltpu.VMEM((8, cols), F32),
                pltpu.VMEM((block_rows, 128), F32),
                pltpu.VMEM((3 * block_rows, atoms), BF16),
                pltpu.VMEM((3, 3 * block_rows, TILE), F32),
                pltpu.VMEM((3, 3 * block_rows, TILE), F32),
                pltpu.VMEM((local, cols), BF16),
                pltpu.VMEM((local, cols), BF16),
                pltpu.VMEM((2 * vecs + 16, cols), BF16),
                pltpu.VMEM((n, 8, vecs), F32),
                pltpu.VMEM((n, vecs + 8, block_rows), F32),
                pltpu.VMEM((n, vecs + 8, block_rows), F32),
                pltpu.VMEM((n, vecs + 8, block_rows), F32),
                pltpu.VMEM((vecs + 8, local), F32),
                pltpu.VMEM((2 * vecs + 16, local), BF16),
                pltpu.VMEM((nr, vecs, 256), F32),
                pltpu.VMEM((nr, vecs + 8, chunk), F32),
                pltpu.VMEM((nr, vecs + 8, chunk), F32),
                pltpu.VMEM((nr, vecs, chunk), F32),
                dma((3, n)), dma((n,)), dma((n,)), dma((n,)), dma((n,)), dma((n,)), dma((n,)), dma((n,)),
                dma((nr,)), dma((nr,)), dma((nr,)), dma((nr,)), dma((nr,)), dma((nr,)),
            ],
            compiler_params=pltpu.CompilerParams(
                collective_id=0, has_side_effects=True, vmem_limit_bytes=48 * 1024 * 1024
            ),
        )(row_coords, col_coords, start_block.T)
        return (basis.T, image.T)

    in_specs = (P(None, ("row", "col"), None), P(None, "col", None), P("col", None))
    out_specs = (P("row", None), P("col", None))
    return jax.shard_map(body, mesh=mesh, in_specs=in_specs, out_specs=out_specs, check_vma=False)
```

time: 303 us -> 110 us (0.36)
  waiting for transfers between devices: 160 us -> 0 us
  Pallas kernels: 0 us -> 103 us
  other arithmetic: 62.7 us -> 0 us
  matrix products: 31.9 us -> 0 us
  blocking collectives: 30.5 us -> 0 us
  between operations: 13.9 us -> 0.65 us
  local copies, waits for them, and re-layouts: 0.54 us -> 5.23 us
    psum x2 -> x0, waiting for transfers between devices: 105 us -> none  [the longest x1 73.1 us: body(): summed = lax.psum((panel_terms[0], panel_terms[1]), 'col')]
    pallas_call x0 -> x1, Pallas kernels: none -> 103 us  [body(): pl.pallas_call(functools.partial(kernel, n, nr, local * nr, cols * n), ou...]
    all_gather x1 -> x0, waiting for transfers between devices: 55 us -> none  [body(): lax.all_gather(row_coords, 'col', axis=1, tiled=True)]
    reduce_sum x7 -> x0, other arithmetic: 45.8 us -> none  [the longest x1 36.2 us: body(): jnp.sum(dist, axis=1)]
    dot_general x5 -> x0, matrix products: 30.5 us -> none  [the longest x1 16 us: body(): jnp.einsum('ark,bck->abrc', rows, cols, preferred_element_type=jnp.float32)]
    psum x3 -> x0, blocking collectives: 30.5 us -> none  [the longest x1 12.6 us: body(): lax.psum((jnp.dot(product.T, product, precision=highest), jnp.sum(product...]
    another operation x5 -> x0, other arithmetic: 12.1 us -> none  [the longest x3 6.52 us: body(): lower = jnp.linalg.cholesky(gram)]
    unnamed x10 -> x8, local copies, waits for them, and re-layouts: 0.46 us -> 5.23 us
  transfers between devices with their start and end apart: 3 -> 0, of which waited for: 3 -> 0; matrix products, arithmetic and copies ran while one was open for 2% -> 0% of each run, Pallas kernels for 0% -> 0%
where the time goes in v1:
time: 110 us; the launch traced here: 109 us
  Pallas kernels  103 us (94%)
  local copies, waits for them, and re-layouts  5.23 us (5%)
    pallas_call x1, Pallas kernels, body(): pl.pallas_call(functools.partial(kernel, n, nr, local * nr, cols * n), ou...  103 us
    unnamed x8, local copies, waits for them, and re-layouts  5.23 us

profile of v1, /device:TPU:25, one launch (start us, length us, event | category | flops | bytes accessed | tf_op | source)
XLA Modules:
  0.0 109.0 jit_solution(17722437854749951378)
XLA Ops:
  0.6 0.0 copy-start
  0.6 1.9 %copy-done = bf16[3,1024,512]{2,1,0:T(8,128)(2,1)S(1)} copy-done((bf16[3,1024,512]{2,1,0:T(8,128)(2,1)S(1)}, bf16[3,1024,512]{2,1,0:T(8,128)(2,1)}, u32[]{:S(2)}) %copy-start) | copy-done | bytes 3145752
  2.5 0.0 copy-start.1
  2.5 1.0 copy-done.1
  3.5 0.0 copy-start.2
  3.5 0.9 copy-done.2
  4.5 103.1 %shard_map.50 = (f32[64,1024]{1,0:T(8,128)S(1)}, f32[64,1024]{1,0:T(8,128)S(1)}) custom-call(bf16[3,128,512]{2,1,0:T(8,128)(2,1)S(1)} %copy-done.1, bf16[3,1024,512]{2,1,0:T(8,128)(2,1)S(1)} %copy-done, f32[64,1024]{1,0:T(8,128)S(1)} %bitcast.5), custom_call_target="tpu_custom_call" | custom-call | tf_op jit(solution)/shard_map/pallas_call | solution.py:369
  107.5 0.7 copy.7
  108.2 0.7 copy.8
Async XLA Ops:
  0.6 1.9 %copy-start = (bf16[3,1024,512]{2,1,0:T(8,128)(2,1)S(1)}, bf16[3,1024,512]{2,1,0:T(8,128)(2,1)}, u32[]{:S(2)}) copy-start(bf16[3,1024,512]{2,1,0:T(8,128)(2,1)} %col_ref.1) | copy-start | bytes 9437188
  2.5 1.0 copy-start.1
  3.5 0.9 copy-start.2

commit v2 on v1

--- a/solution.py
+++ b/solution.py
@@ -49,30 +49,24 @@
     return total, cof, -2.0 * det
 
 
-def distances(items):
-    coeffs = [setup_terms(s) for s, _, _ in items]
-    sums = [rn + cn for _, rn, cn in items]
-    lam = [0.5 * v for v in sums]
-    for _ in range(NEWTON):
-        for k, (total, cof, g) in enumerate(coeffs):
-            x = lam[k]
-            m = x * x - total
-            value = 0.25 * (m * m) + (g * x - cof)
-            lam[k] = x - value * pl.reciprocal(m * x + g, approx=True)
-    return [v - 2.0 * x for v, x in zip(sums, lam)]
-
-
-def kernel(n, nr, total_rows, total_cols, row_ref, col_ref, st_ref, basis_ref, image_ref,
-           rbuf, cc, cn_ref, rn_ref, rc, s_a, s_b, d_hi, d_lo, lhs, ssb, pout, part, agb, q_ref, lhs2,
+def newton(coeffs, lam):
+    total, cof, g = coeffs
+    m = lam * lam - total
+    value = 0.25 * (m * m) + (g * lam - cof)
+    return lam - value * pl.reciprocal(m * lam + g, approx=True)
+
+
+def kernel(n, nr, total_rows, total_cols, row_hbm, col_hbm, st_hbm, basis_ref, image_ref,
+           st_ref, rbuf, rraw, cc, cn_ref, rn_ref, s_a, s_b, d_hi, d_lo, lhs, ssb, pout, part, agb, q_ref, lhs2,
            gx, uout, ub, ib,
-           ag_send, ag_recv, ss_send, ss_recv, pa_send, pa_recv, pg_send, pg_recv,
+           in_sem, ag_send, ag_recv, ss_send, ss_recv, pa_send, pa_recv, pg_send, pg_recv,
            gx_send, gx_recv, u_send, u_recv, i_send, i_recv):
     c, r = lax.axis_index("col"), lax.axis_index("row")
     line = n // 2
     z, x = c // 2, c % 2
-    _, block_rows, atoms = row_ref.shape
-    cols = col_ref.shape[1]
-    vecs = st_ref.shape[0]
+    _, block_rows, atoms = row_hbm.shape
+    cols = col_hbm.shape[1]
+    vecs = st_hbm.shape[0]
     chunk = cols // nr
     tiles = cols // TILE
 
@@ -87,12 +81,24 @@
             src_ref=src, dst_ref=dst, send_sem=send, recv_sem=recv, device_id=dev, device_id_type=MESH
         )
 
+    loads = [
+        pltpu.make_async_copy(row_hbm, rraw, in_sem.at[0]),
+        pltpu.make_async_copy(col_hbm, cc, in_sem.at[1]),
+        pltpu.make_async_copy(st_hbm, st_ref, in_sem.at[2]),
+    ]
+    for load in loads:
+        load.start()
+
     barrier = pltpu.get_barrier_semaphore()
     for d in range(1, n):
         pl.semaphore_signal(barrier, inc=1, device_id=col_dev((c + d) % n), device_id_type=MESH)
     for d in range(1, nr):
         pl.semaphore_signal(barrier, inc=1, device_id=row_dev((r + d) % nr), device_id_type=MESH)
-    rbuf[c] = row_ref[...]
+    loads[0].wait()
+    for a in range(3):
+        v = rraw[a].astype(F32)
+        v = (v - jnp.sum(v, axis=1, keepdims=True) * (1.0 / atoms)).astype(BF16).astype(F32)
+        rbuf[c, a] = (v * (1.0 / atoms)).astype(BF16)
     pl.semaphore_wait(barrier, n - 1 + nr - 1)
 
     def hop(block, way):
@@ -113,6 +119,7 @@
 
     hops(z, lambda copy: copy.start())
 
+    loads[2].wait()
     st = st_ref[...]
     st_hi, st_lo = split(st)
     lhs[0:vecs, :] = st_hi
@@ -127,18 +134,19 @@
     for d in range(1, n):
         ss_copy(d).start()
 
+    loads[1].wait()
     step_rows = 128
 
     def centre_cols(k, carry):
         at = pl.ds(pl.multiple_of(k * step_rows, step_rows), step_rows)
         squares = jnp.zeros((step_rows, atoms), F32)
         for b in range(3):
-            v = col_ref[b, at, :].astype(F32)
+            v = cc[b, at, :].astype(F32)
             v = (v - jnp.sum(v, axis=1, keepdims=True) * (1.0 / atoms)).astype(BF16)
             cc[b, at, :] = v
             v = v.astype(F32)
             squares = squares + v * v
-        cn_ref[:, at] = dot_nt(jnp.ones((8, atoms), F32), squares, HIGHEST) * (1.0 / atoms)
+        cn_ref[:, at] = dot_nt(jnp.ones((8, atoms), F32), squares, HIGHEST) * (0.5 / atoms)
         return carry
 
     lax.fori_loop(0, cols // step_rows, centre_cols, 0)
@@ -153,71 +161,101 @@
     def part_copy(block):
         return remote(pout.at[block], part.at[c], pa_send.at[block], pa_recv.at[c], col_dev(block))
 
-    def run_block(p, carry):
-        block_z = line_place(p // 2)
-        other = p % 2
-        block = block_z * 2 + jnp.where(other == 1, 1 - x, x)
-
-        @pl.when(p > 0)
-        def _():
-            hop(block, 0).wait_recv()
-
-        @pl.when((p > 0) & (other == 0))
-        def _():
-            hops(block_z, lambda copy: copy.start())
-
-        norm = jnp.zeros((block_rows, 1), F32)
+    def block_at(p):
+        return line_place(p // 2) * 2 + jnp.where(p % 2 == 1, 1 - x, x)
+
+    def norms(block, slot):
+        squares = jnp.zeros((block_rows, atoms), F32)
         for a in range(3):
             v = rbuf[block, a].astype(F32)
-            v = (v - jnp.sum(v, axis=1, keepdims=True) * (1.0 / atoms)).astype(BF16).astype(F32)
-            norm = norm + jnp.sum(v * v, axis=1, keepdims=True)
-            rc[a * block_rows:(a + 1) * block_rows, :] = (v * (1.0 / atoms)).astype(BF16)
-        rn_ref[...] = jnp.broadcast_to(norm * (1.0 / atoms), (block_rows, 128))
-
-        def cross(t, out):
-            at = pl.ds(pl.multiple_of(t * TILE, TILE), TILE)
-            for b in range(3):
-                out[b] = dot_nt(rc[...], cc[b, at, :])
-
-        def solve(t, src):
-            for i0 in range(0, block_rows, 32):
-                items, places = [], []
-                for i in range(i0, i0 + 32, 8):
-                    rn = rn_ref[i:i + 8, :]
-                    for l in range(0, TILE, 128):
-                        s = [[src[b, a * block_rows + i:a * block_rows + i + 8, l:l + 128] for b in range(3)]
-                             for a in range(3)]
-                        cn = cn_ref[:, pl.ds(pl.multiple_of(t * TILE + l, 128), 128)]
-                        items.append((s, rn, cn))
-                        places.append((i, l))
-                dist = dict(zip(places, distances(items)))
-                for i in range(i0, i0 + 32, 16):
+            squares = squares + v * v
+        norm = jnp.sum(squares, axis=1, keepdims=True) * (0.5 * atoms)
+        rn_ref[slot] = jnp.broadcast_to(norm, (block_rows, 128))
+
+    def cross(block, t, out):
+        at = pl.ds(pl.multiple_of(t * TILE, TILE), TILE)
+        rows = rbuf[block].reshape(3 * block_rows, atoms)
+        for b in range(3):
+            out[b] = dot_nt(rows, cc[b, at, :])
+
+    groups = [
+        [(i, l) for i in range(i0, i0 + 32, 8) for l in range(0, TILE, 128)]
+        for i0 in range(0, block_rows, 32)
+    ]
+
+    def solve_pair(block, slot, t, between):
+        def half(tile, i, l):
+            cn = cn_ref[:, pl.ds(pl.multiple_of(tile * TILE + l, 128), 128)]
+            return rn_ref[slot, i:i + 8, :] + cn
+
+        def coeffs(src, i, l):
+            at = [slice(a * block_rows + i, a * block_rows + i + 8) for a in range(3)]
+            return setup_terms([[src[b, at[a], l:l + 128] for b in range(3)] for a in range(3)])
+
+        stream = [(t, s_a, g) for g in groups] + [(t + 1, s_b, g) for g in groups]
+        ready = [coeffs(s_a, i, l) for i, l in groups[0]]
+        for index, (tile, _, group) in enumerate(stream):
+            after = stream[index + 1] if index + 1 < len(stream) else None
+            lam = [half(tile, i, l) for i, l in group]
+            upcoming = []
+            for step in range(NEWTON):
+                lam = [newton(ready[k], lam[k]) for k in range(len(group))]
+                if after is not None and step < len(after[2]):
+                    upcoming.append(coeffs(after[1], *after[2][step]))
+            if index == len(groups) - 1:
+                between()
+            dist = {place: half(tile, *place) - v for place, v in zip(group, lam)}
+            for i, l in group:
+                if i % 16 == 0:
+                    value = jnp.concatenate([dist[(i, l)], dist[(i + 8, l)]], axis=0)
                     at_rows = pl.ds(pl.multiple_of(block * block_rows + i, 16), 16)
-                    for l in range(0, TILE, 128):
-                        value = jnp.concatenate([dist[(i, l)], dist[(i + 8, l)]], axis=0)
-                        high, low = split(value)
-                        at_cols = pl.ds(pl.multiple_of(t * TILE + l, 128), 128)
-                        d_hi[at_rows, at_cols] = high
-                        d_lo[at_rows, at_cols] = low
-
-        cross(0, s_a)
+                    at_cols = pl.ds(pl.multiple_of(tile * TILE + l, 128), 128)
+                    high, low = split(value)
+                    d_hi[at_rows, at_cols] = high
+                    d_lo[at_rows, at_cols] = low
+            ready = upcoming
+
+    def run_block(p, carry):
+        block = block_at(p)
+        coming = block_at(jnp.minimum(p + 1, n - 1))
+        slot = p % 2
+
+        @pl.when((p % 2 == 1) & (p < n - 1))
+        def _():
+            far = (p + 1) // 2
+            for place in (z + far, z - far):
+                @pl.when((place >= 0) & (place < line))
+                def _():
+                    hop(place * 2 + x, 0).wait_recv()
+                    hops(place, lambda copy: copy.start())
 
         def pair(k, inner):
             t = 2 * k
-            cross(t + 1, s_b)
-            solve(t, s_a)
-            cross((t + 2) % tiles, s_a)
-            solve(t + 1, s_b)
+            last = k == tiles // 2 - 1
+
+            @pl.when(last & (p < n - 1))
+            def _():
+                @pl.when(p % 2 == 0)
+                def _():
+                    hop(coming, 0).wait_recv()
+
+                norms(coming, 1 - slot)
+
+            cross(block, t + 1, s_b)
+            solve_pair(
+                block, slot, t,
+                lambda: cross(jnp.where(last, coming, block), jnp.where(last, 0, t + 2), s_a),
+            )
             return inner
 
         lax.fori_loop(0, tiles // 2, pair, 0)
 
         at = pl.ds(pl.multiple_of(block * block_rows, block_rows), block_rows)
         high = dot_nt(lhs[...], d_hi[at, :])
-        low = dot_nt(lhs[0:vecs, :], d_lo[at, :])
-        low_sum = dot_nt(lhs[2 * vecs:2 * vecs + 16, :], d_lo[at, :])
-        pout[block, 0:vecs] = high[0:vecs] + high[vecs:2 * vecs] + low
-        pout[block, vecs:vecs + 8] = high[2 * vecs:2 * vecs + 8] + low_sum[0:8]
+        low = dot_nt(lhs[...], d_lo[at, :])
+        both = high + low
+        pout[block, 0:vecs] = both[0:vecs] + both[vecs:2 * vecs]
+        pout[block, vecs:vecs + 8] = both[2 * vecs:2 * vecs + 8]
 
         @pl.when(block == c)
         def _():
@@ -229,6 +267,8 @@
 
         return carry
 
+    norms(c, 0)
+    cross(c, 0, s_a)
     lax.fori_loop(0, n, run_block, 0)
 
     for d in range(1, n):
@@ -286,10 +326,9 @@
         o = (r + d) % nr
         at = pl.ds(pl.multiple_of(o * chunk, chunk), chunk)
         high = dot_nn(lhs2[...], d_hi[:, at])
-        low = dot_nn(lhs2[0:vecs, :], d_lo[:, at])
-        low_sum = dot_nn(lhs2[2 * vecs:2 * vecs + 16, :], d_lo[:, at])
-        product = high[0:vecs] + high[vecs:2 * vecs] + low
-        sums = high[2 * vecs:2 * vecs + 8] + low_sum[0:8]
+        both = high + dot_nn(lhs2[...], d_lo[:, at])
+        product = both[0:vecs] + both[vecs:2 * vecs]
+        sums = both[2 * vecs:2 * vecs + 8]
         if d:
             uout[d, 0:vecs] = product
             uout[d, vecs:vecs + 8] = sums
@@ -332,7 +371,7 @@
     gathered = jnp.broadcast_to(weighted * (-1.0 / total_cols), (vecs, chunk))
     for k in range(nr):
         gathered = gathered + (ub[k, 0:vecs] + (means[k] - mean) * ub[k, vecs:vecs + 1])
-    ib[r] = dot_nn(inverse, gathered, HIGHEST) * (0.5 / math.sqrt(total_rows))
+    ib[r] = dot_nn(inverse, gathered, HIGHEST) * (1.0 / math.sqrt(total_rows))
 
     def i_copy(d):
         return remote(ib.at[r], ib.at[r], i_send.at[d], i_recv.at[r], row_dev((r + d) % nr))
@@ -372,14 +411,15 @@
                 jax.ShapeDtypeStruct((vecs, local), F32),
                 jax.ShapeDtypeStruct((vecs, cols), F32),
             ),
-            in_specs=[pl.BlockSpec(memory_space=pltpu.VMEM)] * 3,
+            in_specs=[pl.BlockSpec(memory_space=pl.ANY)] * 3,
             out_specs=[pl.BlockSpec(memory_space=pltpu.VMEM)] * 2,
             scratch_shapes=[
+                pltpu.VMEM((vecs, cols), F32),
                 pltpu.VMEM((n, 3, block_rows, atoms), BF16),
+                pltpu.VMEM((3, block_rows, atoms), BF16),
                 pltpu.VMEM((3, cols, atoms), BF16),
                 pltpu.VMEM((8, cols), F32),
-                pltpu.VMEM((block_rows, 128), F32),
-                pltpu.VMEM((3 * block_rows, atoms), BF16),
+                pltpu.VMEM((2, block_rows, 128), F32),
                 pltpu.VMEM((3, 3 * block_rows, TILE), F32),
                 pltpu.VMEM((3, 3 * block_rows, TILE), F32),
                 pltpu.VMEM((local, cols), BF16),
@@ -395,11 +435,11 @@
                 pltpu.VMEM((nr, vecs + 8, chunk), F32),
                 pltpu.VMEM((nr, vecs + 8, chunk), F32),
                 pltpu.VMEM((nr, vecs, chunk), F32),
-                dma((3, n)), dma((n,)), dma((n,)), dma((n,)), dma((n,)), dma((n,)), dma((n,)), dma((n,)),
+                dma((3,)), dma((3, n)), dma((n,)), dma((n,)), dma((n,)), dma((n,)), dma((n,)), dma((n,)), dma((n,)),
                 dma((nr,)), dma((nr,)), dma((nr,)), dma((nr,)), dma((nr,)), dma((nr,)),
             ],
             compiler_params=pltpu.CompilerParams(
-                collective_id=0, has_side_effects=True, vmem_limit_bytes=48 * 1024 * 1024
+                collective_id=0, has_side_effects=True, vmem_limit_bytes=56 * 1024 * 1024
             ),
         )(row_coords, col_coords, start_block.T)
         return (basis.T, image.T)

time: 110 us -> 88.5 us (0.80)
  Pallas kernels: 103 us -> 84.1 us
  local copies, waits for them, and re-layouts: 5.23 us -> 3.34 us
    pallas_call x1, Pallas kernels: 103 us -> 84.1 us  [body(): pl.pallas_call(functools.partial(kernel, n, nr, local * nr, cols * n), ou...]
    unnamed x8 -> x2, local copies, waits for them, and re-layouts: 5.23 us -> 3.34 us
where the time goes in v2:
time: 88.5 us; the launch traced here: 88 us
  Pallas kernels  84.1 us (95%)
  local copies, waits for them, and re-layouts  3.34 us (4%)
    pallas_call x1, Pallas kernels, body(): pl.pallas_call(functools.partial(kernel, n, nr, local * nr, cols * n), ou...  84.1 us
    unnamed x2, local copies, waits for them, and re-layouts  3.34 us

profile of v2, /device:TPU:25, one launch (start us, length us, event | category | flops | bytes accessed | tf_op | source)
XLA Modules:
  0.0 88.0 jit_solution(4984779859546985953)
XLA Ops:
  0.6 84.1 %shard_map.50 = (f32[64,1024]{1,0:T(8,128)}, f32[64,1024]{1,0:T(8,128)}) custom-call(bf16[3,128,512]{2,1,0:T(8,128)(2,1)} %row_hbm.1, bf16[3,1024,512]{2,1,0:T(8,128)(2,1)} %col_hbm.1, f32[64,1024]{1,0:T(8,128)} %bitcast.5), custom_call_target="tpu_custom_call" | custom-call | tf_op jit(solution)/shard_map/pallas_call | solution.py:408
  84.7 1.7 %copy.7 = f32[1024,64]{0,1:T(8,128)} copy(f32[1024,64]{0,1:T(8,128)} %bitcast.4) | data formatting | bytes 524288
  86.4 1.7 %copy.8 = f32[1024,64]{0,1:T(8,128)} copy(f32[1024,64]{0,1:T(8,128)} %bitcast.3) | data formatting | bytes 524288

commit v3 on v2

--- a/solution.py
+++ b/solution.py
@@ -57,7 +57,7 @@
 
 
 def kernel(n, nr, total_rows, total_cols, row_hbm, col_hbm, st_hbm, basis_ref, image_ref,
-           st_ref, rbuf, rraw, cc, cn_ref, rn_ref, s_a, s_b, d_hi, d_lo, lhs, ssb, pout, part, agb, q_ref, lhs2,
+           st_ref, rbuf, rraw, craw, cc, cn_ref, rn_ref, s_a, s_b, d_hi, d_lo, start, ssb, pout, part, agb, q_ref, lhs2,
            gx, uout, ub, ib,
            in_sem, ag_send, ag_recv, ss_send, ss_recv, pa_send, pa_recv, pg_send, pg_recv,
            gx_send, gx_recv, u_send, u_recv, i_send, i_recv):
@@ -83,7 +83,7 @@
 
     loads = [
         pltpu.make_async_copy(row_hbm, rraw, in_sem.at[0]),
-        pltpu.make_async_copy(col_hbm, cc, in_sem.at[1]),
+        pltpu.make_async_copy(col_hbm, craw, in_sem.at[1]),
         pltpu.make_async_copy(st_hbm, st_ref, in_sem.at[2]),
     ]
     for load in loads:
@@ -120,12 +120,12 @@
     hops(z, lambda copy: copy.start())
 
     loads[2].wait()
-    st = st_ref[...]
+    st = st_ref[...].T
     st_hi, st_lo = split(st)
-    lhs[0:vecs, :] = st_hi
-    lhs[vecs:2 * vecs, :] = st_lo
-    lhs[2 * vecs:2 * vecs + 16, :] = jnp.ones((16, cols), BF16)
-    ssb[c] = dot_nt(jnp.ones((8, cols), F32), st, HIGHEST)
+    start[:, 0:vecs] = st_hi
+    start[:, vecs:2 * vecs] = st_lo
+    start[:, 2 * vecs:] = jnp.ones((cols, 128), BF16)
+    ssb[c] = jnp.broadcast_to(jnp.sum(st, axis=0, keepdims=True), (8, vecs))
 
     def ss_copy(d):
         k = (c + d) % n
@@ -139,14 +139,16 @@
 
     def centre_cols(k, carry):
         at = pl.ds(pl.multiple_of(k * step_rows, step_rows), step_rows)
-        squares = jnp.zeros((step_rows, atoms), F32)
+        squares = jnp.zeros((atoms, step_rows), F32)
         for b in range(3):
-            v = cc[b, at, :].astype(F32)
-            v = (v - jnp.sum(v, axis=1, keepdims=True) * (1.0 / atoms)).astype(BF16)
-            cc[b, at, :] = v
+            v = craw[b, at, :].astype(F32)
+            v = v - jnp.sum(v, axis=1, keepdims=True) * (1.0 / atoms)
+            v = v.T.astype(BF16)
+            cc[b, :, at] = v
             v = v.astype(F32)
             squares = squares + v * v
-        cn_ref[:, at] = dot_nt(jnp.ones((8, atoms), F32), squares, HIGHEST) * (0.5 / atoms)
+        norm = jnp.sum(squares, axis=0, keepdims=True) * (0.5 / atoms)
+        cn_ref[:, at] = jnp.broadcast_to(norm, (8, step_rows))
         return carry
 
     lax.fori_loop(0, cols // step_rows, centre_cols, 0)
@@ -176,7 +178,7 @@
         at = pl.ds(pl.multiple_of(t * TILE, TILE), TILE)
         rows = rbuf[block].reshape(3 * block_rows, atoms)
         for b in range(3):
-            out[b] = dot_nt(rows, cc[b, at, :])
+            out[b] = dot_nn(rows, cc[b, :, at])
 
     groups = [
         [(i, l) for i in range(i0, i0 + 32, 8) for l in range(0, TILE, 128)]
@@ -251,9 +253,7 @@
         lax.fori_loop(0, tiles // 2, pair, 0)
 
         at = pl.ds(pl.multiple_of(block * block_rows, block_rows), block_rows)
-        high = dot_nt(lhs[...], d_hi[at, :])
-        low = dot_nt(lhs[...], d_lo[at, :])
-        both = high + low
+        both = (dot_nn(d_hi[at, :], start[...]) + dot_nn(d_lo[at, :], start[...])).T
         pout[block, 0:vecs] = both[0:vecs] + both[vecs:2 * vecs]
         pout[block, vecs:vecs + 8] = both[2 * vecs:2 * vecs + 8]
 
@@ -411,20 +411,21 @@
                 jax.ShapeDtypeStruct((vecs, local), F32),
                 jax.ShapeDtypeStruct((vecs, cols), F32),
             ),
-            in_specs=[pl.BlockSpec(memory_space=pl.ANY)] * 3,
+            in_specs=[pl.BlockSpec(memory_space=pltpu.HBM)] * 3,
             out_specs=[pl.BlockSpec(memory_space=pltpu.VMEM)] * 2,
             scratch_shapes=[
                 pltpu.VMEM((vecs, cols), F32),
                 pltpu.VMEM((n, 3, block_rows, atoms), BF16),
                 pltpu.VMEM((3, block_rows, atoms), BF16),
                 pltpu.VMEM((3, cols, atoms), BF16),
+                pltpu.VMEM((3, atoms, cols), BF16),
                 pltpu.VMEM((8, cols), F32),
                 pltpu.VMEM((2, block_rows, 128), F32),
                 pltpu.VMEM((3, 3 * block_rows, TILE), F32),
                 pltpu.VMEM((3, 3 * block_rows, TILE), F32),
                 pltpu.VMEM((local, cols), BF16),
                 pltpu.VMEM((local, cols), BF16),
-                pltpu.VMEM((2 * vecs + 16, cols), BF16),
+                pltpu.VMEM((cols, 2 * vecs + 128), BF16),
                 pltpu.VMEM((n, 8, vecs), F32),
                 pltpu.VMEM((n, vecs + 8, block_rows), F32),
                 pltpu.VMEM((n, vecs + 8, block_rows), F32),
@@ -439,7 +440,7 @@
                 dma((nr,)), dma((nr,)), dma((nr,)), dma((nr,)), dma((nr,)), dma((nr,)),
             ],
             compiler_params=pltpu.CompilerParams(
-                collective_id=0, has_side_effects=True, vmem_limit_bytes=56 * 1024 * 1024
+                collective_id=0, has_side_effects=True, vmem_limit_bytes=54500 * 1024
             ),
         )(row_coords, col_coords, start_block.T)
         return (basis.T, image.T)

time: 88.5 us -> 86 us (0.972)
  local copies, waits for them, and re-layouts: 3.34 us -> 1.41 us
    unnamed x2, local copies, waits for them, and re-layouts: 3.34 us -> 1.41 us
where the time goes in v3:
time: 86 us; the launch traced here: 85.6 us
  Pallas kernels  83.5 us (97%)
  local copies, waits for them, and re-layouts  1.41 us (2%)
    pallas_call x1, Pallas kernels, body(): pl.pallas_call(functools.partial(kernel, n, nr, local * nr, cols * n), ou...  83.5 us

profile of v3, /device:TPU:25, one launch (start us, length us, event | category | flops | bytes accessed | tf_op | source)
XLA Modules:
  0.0 85.6 jit_solution(11766132383411936396)
XLA Ops:
  0.6 83.5 %shard_map.50 = (f32[64,1024]{1,0:T(8,128)S(1)}, f32[64,1024]{1,0:T(8,128)S(1)}) custom-call(bf16[3,128,512]{2,1,0:T(8,128)(2,1)} %row_hbm.1, bf16[3,1024,512]{2,1,0:T(8,128)(2,1)} %col_hbm.1, f32[64,1024]{1,0:T(8,128)} %bitcast.5), custom_call_target="tpu_custom_call" | custom-call | tf_op jit(solution)/shard_map/pallas_call | solution.py:408
  84.2 0.7 copy.7
  84.9 0.7 copy.8

commit v4 on v3

--- a/solution.py
+++ b/solution.py
@@ -101,23 +101,40 @@
         rbuf[c, a] = (v * (1.0 / atoms)).astype(BF16)
     pl.semaphore_wait(barrier, n - 1 + nr - 1)
 
-    def hop(block, way):
+    half_rows = block_rows // 2
+
+    def hop(block, half, way):
         dev = col_dev((c + 1 - 2 * x, c + 2, c - 2)[way])
-        return remote(rbuf.at[block], rbuf.at[block], ag_send.at[way, block], ag_recv.at[block], dev)
-
-    def hops(block_z, act):
-        block = block_z * 2 + x
-        act(hop(block, 0))
-
-        @pl.when((block_z <= z) & (z < line - 1))
+        piece = rbuf.at[block, :, half * half_rows:(half + 1) * half_rows, :]
+        return remote(piece, piece, ag_send.at[way, half, block], ag_recv.at[half, block], dev)
+
+    def is_end(place):
+        return (place == 0) | (place == line - 1)
+
+    def line_hops(block, place, half, act):
+        @pl.when((place <= z) & (z < line - 1))
         def _():
-            act(hop(block, 1))
-
-        @pl.when((block_z >= z) & (z > 0))
+            act(hop(block, half, 1))
+
+        @pl.when((place >= z) & (z > 0))
         def _():
-            act(hop(block, 2))
-
-    hops(z, lambda copy: copy.start())
+            act(hop(block, half, 2))
+
+    def hops(place, act):
+        block = place * 2 + x
+        for half in range(2):
+            line_hops(block, place, half, act)
+        act(hop(block, 0, 0))
+
+        @pl.when(jnp.logical_not(is_end(place)) | (place == z))
+        def _():
+            act(hop(block, 1, 0))
+
+    def crossed_hops(place, act):
+        line_hops(place * 2 + 1 - x, place, 1, act)
+
+    start_copy = lambda copy: copy.start()
+    hops(z, start_copy)
 
     loads[2].wait()
     st = st_ref[...].T
@@ -222,14 +239,38 @@
         coming = block_at(jnp.minimum(p + 1, n - 1))
         slot = p % 2
 
-        @pl.when((p % 2 == 1) & (p < n - 1))
-        def _():
-            far = (p + 1) // 2
-            for place in (z + far, z - far):
-                @pl.when((place >= 0) & (place < line))
+        def fetch():
+            far = p // 2 + 1
+
+            @pl.when((p % 2 == 0) & (far < line))
+            def _():
+                for place in (z + far, z - far):
+                    @pl.when((place >= 0) & (place < line))
+                    def _():
+                        hop(place * 2 + x, 0, 0).wait_recv()
+                        hop(place * 2 + x, 1, 0).wait_recv()
+                        hops(place, start_copy)
+
+            @pl.when(p % 2 == 0)
+            def _():
+                place = line_place(p // 2)
+                hop(coming, 0, 0).wait_recv()
+
+                @pl.when(jnp.logical_not(is_end(place)) | (place == z))
                 def _():
-                    hop(place * 2 + x, 0).wait_recv()
-                    hops(place, lambda copy: copy.start())
+                    hop(coming, 1, 0).wait_recv()
+
+                @pl.when(is_end(place) & (place == z))
+                def _():
+                    crossed_hops(place, start_copy)
+
+            @pl.when((p % 2 == 1) & (far < line))
+            def _():
+                for place, end in ((z + far, line - 1), (z - far, 0)):
+                    @pl.when(place == end)
+                    def _():
+                        hop(place * 2 + 1 - x, 1, 0).wait_recv()
+                        crossed_hops(place, start_copy)
 
         def pair(k, inner):
             t = 2 * k
@@ -237,10 +278,7 @@
 
             @pl.when(last & (p < n - 1))
             def _():
-                @pl.when(p % 2 == 0)
-                def _():
-                    hop(coming, 0).wait_recv()
-
+                fetch()
                 norms(coming, 1 - slot)
 
             cross(block, t + 1, s_b)
@@ -353,14 +391,19 @@
 
     work = jnp.concatenate([gram, jnp.where(eye, 1.0, 0.0)], axis=1)
     below = lax.broadcasted_iota(jnp.int32, (vecs, 1), 0)
-    pivots = jnp.zeros((vecs, 1), F32)
-    for k in range(vecs):
-        top = work[k:k + 1, :]
-        pivot = top[:, k:k + 1]
-        pivots = jnp.where(below == k, pivot, pivots)
-        factor = jnp.where(below > k, work[:, k:k + 1], 0.0)
-        work = work - factor * (top * (1.0 / pivot))
-    inverse = work[:, vecs:2 * vecs] * lax.rsqrt(pivots)
+    ratio, scale = jnp.zeros((vecs, 1), F32), jnp.zeros((vecs, 1), F32)
+    for k in range(0, vecs, 2):
+        top, low = work[k:k + 1, :], work[k + 1:k + 2, :]
+        left, right = work[:, k:k + 1], work[:, k + 1:k + 2]
+        first, off, second = top[:, k:k + 1], top[:, k + 1:k + 2], low[:, k + 1:k + 2]
+        inv = 1.0 / (first * second - off * off)
+        ratio = jnp.where(below == k + 1, off / first, ratio)
+        scale = jnp.where(below == k, first, jnp.where(below == k + 1, second - off * (off / first), scale))
+        keep = jnp.where(below > k + 1, inv, 0.0)
+        work = work - ((left * second - right * off) * keep) * top - ((right * first - left * off) * keep) * low
+    unit = work[:, vecs:2 * vecs]
+    above = jnp.concatenate([unit[vecs - 1:vecs, :], unit[0:vecs - 1, :]], axis=0)
+    inverse = (unit - ratio * above) * lax.rsqrt(scale)
 
     own_mean = jnp.sum(jnp.where(lane == r, shift, 0.0), axis=1, keepdims=True)
     basis_ref[...] = -dot_nn(inverse, q_ref[0:vecs, :] + own_mean, HIGHEST)
@@ -386,6 +429,8 @@
 
     for place in range(line):
         hops(place, lambda copy: copy.wait_send())
+    for place in (0, line - 1):
+        crossed_hops(place, lambda copy: copy.wait_send())
     for d in range(1, n):
         ss_copy(d).wait_send()
         pg_copy(d).wait_send()
@@ -436,7 +481,7 @@
                 pltpu.VMEM((nr, vecs + 8, chunk), F32),
                 pltpu.VMEM((nr, vecs + 8, chunk), F32),
                 pltpu.VMEM((nr, vecs, chunk), F32),
-                dma((3,)), dma((3, n)), dma((n,)), dma((n,)), dma((n,)), dma((n,)), dma((n,)), dma((n,)), dma((n,)),
+                dma((3,)), dma((3, 2, n)), dma((2, n)), dma((n,)), dma((n,)), dma((n,)), dma((n,)), dma((n,)), dma((n,)),
                 dma((nr,)), dma((nr,)), dma((nr,)), dma((nr,)), dma((nr,)), dma((nr,)),
             ],
             compiler_params=pltpu.CompilerParams(

time: 86 us -> 85.1 us (0.990)
  no operation moved by 1% of the time
where the time goes in v4:
time: 85.1 us; the launch traced here: 85 us
  Pallas kernels  82.9 us (97%)
  local copies, waits for them, and re-layouts  1.41 us (2%)
    pallas_call x1, Pallas kernels, body(): pl.pallas_call(functools.partial(kernel, n, nr, local * nr, cols * n), ou...  82.9 us

profile of v4, /device:TPU:25, one launch (start us, length us, event | category | flops | bytes accessed | tf_op | source)
XLA Modules:
  0.0 85.0 jit_solution(15994860732468044551)
XLA Ops:
  0.6 82.9 %shard_map.50 = (f32[64,1024]{1,0:T(8,128)S(1)}, f32[64,1024]{1,0:T(8,128)S(1)}) custom-call(bf16[3,128,512]{2,1,0:T(8,128)(2,1)} %row_hbm.1, bf16[3,1024,512]{2,1,0:T(8,128)(2,1)} %col_hbm.1, f32[64,1024]{1,0:T(8,128)} %bitcast.5), custom_call_target="tpu_custom_call" | custom-call | tf_op jit(solution)/shard_map/pallas_call | solution.py:453
  83.5 0.7 copy.7
  84.3 0.7 copy.8

commit v5 on v4

--- a/solution.py
+++ b/solution.py
@@ -49,15 +49,28 @@
     return total, cof, -2.0 * det
 
 
-def newton(coeffs, lam):
-    total, cof, g = coeffs
-    m = lam * lam - total
-    value = 0.25 * (m * m) + (g * lam - cof)
-    return lam - value * pl.reciprocal(m * lam + g, approx=True)
+def newton(coeffs, lam, beside):
+    every = range(len(lam))
+    totals = [coeffs(0, k) for k in every]
+    squares = [lam[k] * lam[k] for k in every]
+    m = [squares[k] - totals[k] for k in every]
+    g = [coeffs(2, k) for k in every]
+    slope = [m[k] * lam[k] for k in every]
+    slope = [slope[k] + g[k] for k in every]
+    inverse = [pl.reciprocal(slope[k], approx=True) for k in every]
+    linear = [g[k] * lam[k] for k in every]
+    cof = [coeffs(1, k) for k in every]
+    linear = [linear[k] - cof[k] for k in every]
+    quarter = [0.25 * m[k] for k in every]
+    value = [quarter[k] * m[k] for k in every]
+    value = [value[k] + linear[k] for k in every]
+    beside()
+    step = [value[k] * inverse[k] for k in every]
+    return [lam[k] - step[k] for k in every]
 
 
 def kernel(n, nr, total_rows, total_cols, row_hbm, col_hbm, st_hbm, basis_ref, image_ref,
-           st_ref, rbuf, rraw, craw, cc, cn_ref, rn_ref, s_a, s_b, d_hi, d_lo, start, ssb, pout, part, agb, q_ref, lhs2,
+           st_ref, rbuf, rraw, craw, cc, cn_ref, rn_ref, co_ref, s_a, s_b, d_hi, d_lo, start, ssb, pout, part, agb, q_ref, lhs2,
            gx, uout, ub, ib,
            in_sem, ag_send, ag_recv, ss_send, ss_recv, pa_send, pa_recv, pg_send, pg_recv,
            gx_send, gx_recv, u_send, u_recv, i_send, i_recv):
@@ -191,10 +204,10 @@
         norm = jnp.sum(squares, axis=1, keepdims=True) * (0.5 * atoms)
         rn_ref[slot] = jnp.broadcast_to(norm, (block_rows, 128))
 
-    def cross(block, t, out):
+    def cross(block, t, out, parts=range(3)):
         at = pl.ds(pl.multiple_of(t * TILE, TILE), TILE)
         rows = rbuf[block].reshape(3 * block_rows, atoms)
-        for b in range(3):
+        for b in parts:
             out[b] = dot_nn(rows, cc[b, :, at])
 
     groups = [
@@ -202,27 +215,39 @@
         for i0 in range(0, block_rows, 32)
     ]
 
-    def solve_pair(block, slot, t, between):
+    def solve_pair(block, slot, t, coming, first):
         def half(tile, i, l):
             cn = cn_ref[:, pl.ds(pl.multiple_of(tile * TILE + l, 128), 128)]
             return rn_ref[slot, i:i + 8, :] + cn
 
-        def coeffs(src, i, l):
+        def coeffs(turn, k, src, i, l):
             at = [slice(a * block_rows + i, a * block_rows + i + 8) for a in range(3)]
-            return setup_terms([[src[b, at[a], l:l + 128] for b in range(3)] for a in range(3)])
+            terms = setup_terms([[src[b, at[a], l:l + 128] for b in range(3)] for a in range(3)])
+            for kind in range(3):
+                co_ref[turn, kind, k] = terms[kind]
 
         stream = [(t, s_a, g) for g in groups] + [(t + 1, s_b, g) for g in groups]
-        ready = [coeffs(s_a, i, l) for i, l in groups[0]]
+        for k, (i, l) in enumerate(groups[0]):
+            coeffs(0, k, s_a, i, l)
         for index, (tile, _, group) in enumerate(stream):
             after = stream[index + 1] if index + 1 < len(stream) else None
+            turn = index % 2
+            place = index % len(groups)
+            if index < len(groups):
+                if place < min(3, len(groups) - 1):
+                    cross(block, t + 1, s_b, range(place, 3, max(1, min(3, len(groups) - 1))))
+                elif len(groups) == 1:
+                    cross(block, t + 1, s_b)
+            elif place < min(3, len(groups)):
+                cross(coming, first, s_a, range(place, 3, min(3, len(groups))))
             lam = [half(tile, i, l) for i, l in group]
-            upcoming = []
             for step in range(NEWTON):
-                lam = [newton(ready[k], lam[k]) for k in range(len(group))]
-                if after is not None and step < len(after[2]):
-                    upcoming.append(coeffs(after[1], *after[2][step]))
-            if index == len(groups) - 1:
-                between()
+
+                def beside():
+                    if after is not None and step < len(after[2]):
+                        coeffs(1 - turn, step, after[1], *after[2][step])
+
+                lam = newton(lambda kind, k: co_ref[turn, kind, k], lam, beside)
             dist = {place: half(tile, *place) - v for place, v in zip(group, lam)}
             for i, l in group:
                 if i % 16 == 0:
@@ -232,7 +257,6 @@
                     high, low = split(value)
                     d_hi[at_rows, at_cols] = high
                     d_lo[at_rows, at_cols] = low
-            ready = upcoming
 
     def run_block(p, carry):
         block = block_at(p)
@@ -281,11 +305,7 @@
                 fetch()
                 norms(coming, 1 - slot)
 
-            cross(block, t + 1, s_b)
-            solve_pair(
-                block, slot, t,
-                lambda: cross(jnp.where(last, coming, block), jnp.where(last, 0, t + 2), s_a),
-            )
+            solve_pair(block, slot, t, jnp.where(last, coming, block), jnp.where(last, 0, t + 2))
             return inner
 
         lax.fori_loop(0, tiles // 2, pair, 0)
@@ -466,6 +486,7 @@
                 pltpu.VMEM((3, atoms, cols), BF16),
                 pltpu.VMEM((8, cols), F32),
                 pltpu.VMEM((2, block_rows, 128), F32),
+                pltpu.VMEM((2, 3, 8, 8, 128), F32),
                 pltpu.VMEM((3, 3 * block_rows, TILE), F32),
                 pltpu.VMEM((3, 3 * block_rows, TILE), F32),
                 pltpu.VMEM((local, cols), BF16),

time: 85.1 us -> 84.9 us (level)
  no operation moved by 1% of the time
where the time goes in v5:
time: 84.9 us; the launch traced here: 84.7 us
  Pallas kernels  82.7 us (97%)
  local copies, waits for them, and re-layouts  1.41 us (2%)
    pallas_call x1, Pallas kernels, body(): pl.pallas_call(functools.partial(kernel, n, nr, local * nr, cols * n), ou...  82.7 us

profile of v5, /device:TPU:25, one launch (start us, length us, event | category | flops | bytes accessed | tf_op | source)
XLA Modules:
  0.0 84.7 jit_solution(10393312075256481303)
XLA Ops:
  0.6 82.7 %shard_map.50 = (f32[64,1024]{1,0:T(8,128)S(1)}, f32[64,1024]{1,0:T(8,128)S(1)}) custom-call(bf16[3,128,512]{2,1,0:T(8,128)(2,1)} %row_hbm.1, bf16[3,1024,512]{2,1,0:T(8,128)(2,1)} %col_hbm.1, f32[64,1024]{1,0:T(8,128)} %bitcast.5), custom_call_target="tpu_custom_call" | custom-call | tf_op jit(solution)/shard_map/pallas_call | solution.py:473
  83.3 0.7 copy.7
  84.0 0.7 copy.8

commit v6 on v5

--- a/solution.py
+++ b/solution.py
@@ -70,7 +70,7 @@
 
 
 def kernel(n, nr, total_rows, total_cols, row_hbm, col_hbm, st_hbm, basis_ref, image_ref,
-           st_ref, rbuf, rraw, craw, cc, cn_ref, rn_ref, co_ref, s_a, s_b, d_hi, d_lo, start, ssb, pout, part, agb, q_ref, lhs2,
+           st_ref, rbuf, rraw, craw, cc, cn_ref, rn_ref, co_ref, acc, s_a, s_b, d_hi, d_lo, start, ssb, pout, part, agb, q_ref, lhs2,
            gx, uout, ub, ib,
            in_sem, ag_send, ag_recv, ss_send, ss_recv, pa_send, pa_recv, pg_send, pg_recv,
            gx_send, gx_recv, u_send, u_recv, i_send, i_recv):
@@ -173,7 +173,7 @@
         for b in range(3):
             v = craw[b, at, :].astype(F32)
             v = v - jnp.sum(v, axis=1, keepdims=True) * (1.0 / atoms)
-            v = v.T.astype(BF16)
+            v = v.astype(BF16).T
             cc[b, :, at] = v
             v = v.astype(F32)
             squares = squares + v * v
@@ -258,6 +258,27 @@
                     d_hi[at_rows, at_cols] = high
                     d_lo[at_rows, at_cols] = low
 
+    span = 2 * TILE
+
+    def panel_product(block, first, fresh):
+        at = pl.ds(pl.multiple_of(block * block_rows, block_rows), block_rows)
+        to = pl.ds(pl.multiple_of(first, span), span)
+        value = dot_nn(d_hi[at, to], start[to, :]) + dot_nn(d_lo[at, to], start[to, :])
+        acc[...] = jnp.where(fresh, value, acc[...] + value)
+
+    def hand_over(block):
+        both = acc[...].T
+        pout[block, 0:vecs] = both[0:vecs] + both[vecs:2 * vecs]
+        pout[block, vecs:vecs + 8] = both[2 * vecs:2 * vecs + 8]
+
+        @pl.when(block == c)
+        def _():
+            part[c] = pout[block]
+
+        @pl.when(block != c)
+        def _():
+            part_copy(block).start()
+
     def run_block(p, carry):
         block = block_at(p)
         coming = block_at(jnp.minimum(p + 1, n - 1))
@@ -305,29 +326,26 @@
                 fetch()
                 norms(coming, 1 - slot)
 
+            before = block_at(jnp.maximum(p - 1, 0))
+            opening = k == 0
+            panel_product(jnp.where(opening, before, block), jnp.where(opening, cols - span, (k - 1) * span), (k == 1) | (tiles == 2))
             solve_pair(block, slot, t, jnp.where(last, coming, block), jnp.where(last, 0, t + 2))
+
+            @pl.when(opening & (p > 0))
+            def _():
+                hand_over(before)
+
             return inner
 
         lax.fori_loop(0, tiles // 2, pair, 0)
-
-        at = pl.ds(pl.multiple_of(block * block_rows, block_rows), block_rows)
-        both = (dot_nn(d_hi[at, :], start[...]) + dot_nn(d_lo[at, :], start[...])).T
-        pout[block, 0:vecs] = both[0:vecs] + both[vecs:2 * vecs]
-        pout[block, vecs:vecs + 8] = both[2 * vecs:2 * vecs + 8]
-
-        @pl.when(block == c)
-        def _():
-            part[c] = pout[block]
-
-        @pl.when(block != c)
-        def _():
-            part_copy(block).start()
 
         return carry
 
     norms(c, 0)
     cross(c, 0, s_a)
     lax.fori_loop(0, n, run_block, 0)
+    panel_product(block_at(n - 1), cols - span, tiles == 2)
+    hand_over(block_at(n - 1))
 
     for d in range(1, n):
         k = (c + d) % n
@@ -487,6 +505,7 @@
                 pltpu.VMEM((8, cols), F32),
                 pltpu.VMEM((2, block_rows, 128), F32),
                 pltpu.VMEM((2, 3, 8, 8, 128), F32),
+                pltpu.VMEM((block_rows, 2 * vecs + 128), F32),
                 pltpu.VMEM((3, 3 * block_rows, TILE), F32),
                 pltpu.VMEM((3, 3 * block_rows, TILE), F32),
                 pltpu.VMEM((local, cols), BF16),

time: 84.9 us -> 84.6 us (level)
  no operation moved by 1% of the time
where the time goes in v6:
time: 84.6 us; the launch traced here: 84.5 us
  Pallas kernels  82.4 us (97%)
  local copies, waits for them, and re-layouts  1.41 us (2%)
    pallas_call x1, Pallas kernels, body(): pl.pallas_call(functools.partial(kernel, n, nr, local * nr, cols * n), ou...  82.4 us

profile of v6, /device:TPU:25, one launch (start us, length us, event | category | flops | bytes accessed | tf_op | source)
XLA Modules:
  0.0 84.5 jit_solution(4315038463489854042)
XLA Ops:
  0.6 82.4 %shard_map.50 = (f32[64,1024]{1,0:T(8,128)S(1)}, f32[64,1024]{1,0:T(8,128)S(1)}) custom-call(bf16[3,128,512]{2,1,0:T(8,128)(2,1)} %row_hbm.1, bf16[3,1024,512]{2,1,0:T(8,128)(2,1)} %col_hbm.1, f32[64,1024]{1,0:T(8,128)} %bitcast.5), custom_call_target="tpu_custom_call" | custom-call | tf_op jit(solution)/shard_map/pallas_call | solution.py:491
  83.1 0.7 copy.7
  83.8 0.7 copy.8
